TPU v7x, 32 devices: a whole 2x2x4 slice. The times are simulated.
32 devices in a mesh: seq: 8 (over z, x), tensor: 4 (over y, core).
Axes of the slice: x: 2, y: 2, z: 4, core: 2. Of those that a mesh axis runs over, the one named last changes fastest.
Arguments:
- queries: bfloat16 [512, 2048], P('seq', 'tensor'), may hold values from -5 to 5
- draft_keys: bfloat16 [512, 2048], P('seq', 'tensor'), may hold values from -5 to 5
- draft_values: bfloat16 [512, 2048], P('seq', 'tensor'), may hold values from -6 to 6
- key_cache: bfloat16 [96, 128, 2048], P('seq', None, 'tensor'), may hold values from -6 to 6
- value_cache: bfloat16 [96, 128, 2048], P('seq', None, 'tensor'), may hold values from -6 to 6
- page_request: int32 [96], P('seq'), may hold values from 0 to 7, as said below
- page_slot: int32 [96], P('seq'), may hold values from 0 to 88, as said below
- cache_len: int32 [8], replicated, may hold values from 1 to 11384, as said below
- tree_mask: int32 [8, 64, 64], P('seq'), may hold values from 0 to 1, as said below
- accepted: int32 [8, 8], P('seq'), may hold values from 0 to 28, as said below
- hidden_in: bfloat16 [512, 2048], P('seq'), may hold values from -0.75 to 0.75
- out_proj: bfloat16 [2048, 2048], P('tensor'), may hold values from -0.125 to 0.125
- norm_gain: float32 [2048], replicated, may hold values from 0.5 to 1.5
- gate_proj: bfloat16 [64, 2048, 1024], P('seq', None, 'tensor'), may hold values from -0.125 to 0.125
- up_proj: bfloat16 [64, 2048, 1024], P('seq', None, 'tensor'), may hold values from -0.125 to 0.125
- down_proj: bfloat16 [64, 1024, 2048], P('seq', 'tensor'), may hold values from -0.1875 to 0.1875
- expert_ids: int32 [512, 8], P('seq'), may hold values from 0 to 63, all different within a row; in each aligned block of 64 rows (0 to 63, 64 to 127, ...) at most 16 rows name the same one
- route_weight: float32 [512, 8], P('seq'), may hold values from 0.02 to 0.5
Outputs:
- mixed_out: bfloat16 [512, 2048], P('seq', 'tensor')
- log_sum_exp: float32 [512, 16], P('seq', 'tensor')
- key_cache_out: bfloat16 [96, 128, 2048], P('seq', None, 'tensor')
- value_cache_out: bfloat16 [96, 128, 2048], P('seq', None, 'tensor')
Inputs may be any that keep to these rules, and one draw needn't show every extreme that they name: `page_request`: every request holds one or more pages and at most 128; together they hold all 96 pages, and one request holds min(128, 89). `page_slot`: the pages of one request carry the numbers 0, 1, 2 and so on, each once. A request's pages hold cache_len + 8 positions or more, and its last page holds at least one of its first cache_len positions. `tree_mask`: row i marks node i and its ancestors in a tree rooted at node 0; each node's parent stands one to four nodes before it. `accepted`: the 8 nodes nearest the root on a path from node 0, in order from the root. `expert_ids`: at most 16 of the 64 rows of one request name the same expert.
All inputs are finite; a program needn't handle non-finite values.
Results may differ from a plain program's by a relative error of at most 0.024.
Values may be sent and summed in bfloat16 or wider, within the bound.
No kernel may reach another device: no remote copies, remote signals or barrier semaphores. Data moves between devices by JAX's collectives and lax.ppermute only.
A program may use at most 128 MiB of HBM per device.

v0:
```python
import math
import jax
import jax.numpy as jnp
from jax import lax
from jax.sharding import PartitionSpec as P

HD = 128
EXPERTS = 64
CAP = 16
MASKED = -1e30
HIGHEST = lax.Precision.HIGHEST


def expert_block(slot_rows, gate_proj, up_proj, down_proj):
    gate_value = jnp.einsum(
        "gecd,edf->gecf", slot_rows, gate_proj, preferred_element_type=jnp.float32
    )
    up_value = jnp.einsum("gecd,edf->gecf", slot_rows, up_proj, preferred_element_type=jnp.float32)
    active = (jax.nn.silu(gate_value) * up_value).astype(jnp.bfloat16)
    return jnp.einsum(
        "gecf,efd->gecd", active, down_proj, preferred_element_type=jnp.float32
    ).astype(jnp.bfloat16)


def on_device(
    queries,
    draft_keys,
    draft_values,
    key_cache,
    value_cache,
    page_request,
    page_slot,
    cache_len,
    tree_mask,
    accepted,
    hidden_in,
    out_proj,
    norm_gain,
    gate_proj,
    up_proj,
    down_proj,
    expert_ids,
    route_weight,
):
    draft_len, head_width = queries.shape
    page_count, page_len, _ = key_cache.shape
    head_count = head_width // HD
    scaling = 1.0 / math.sqrt(HD)
    accept_rows = jnp.concatenate([draft_keys[accepted[0]], draft_values[accepted[0]]], axis=1)
    every_query, every_accept = (
        lax.all_gather(queries[None], "seq", axis=0, tiled=True),
        lax.all_gather(accept_rows[None], "seq", axis=0, tiled=True),
    )
    request_count = every_query.shape[0]
    request_ids = jnp.arange(request_count, dtype=jnp.int32)
    owner_mask = page_request[:, None] == request_ids[None, :]
    owner_weight = owner_mask.astype(jnp.bfloat16)
    page_queries = jnp.einsum(
        "pr,rqc->pqc", owner_weight, every_query, preferred_element_type=jnp.float32
    ).astype(jnp.bfloat16)
    page_length = jnp.sum(jnp.where(owner_mask, cache_len[None, :], 0), axis=1)
    position = page_slot[:, None] * page_len + jnp.arange(page_len, dtype=jnp.int32)[None, :]
    live_key = position < page_length[:, None]
    far_scores = (
        jnp.einsum(
            "pqhd,pkhd->phqk",
            page_queries.reshape(page_count, draft_len, head_count, HD),
            key_cache.reshape(page_count, page_len, head_count, HD),
            preferred_element_type=jnp.float32,
        )
        * scaling
    )
    far_scores = jnp.where(live_key[:, None, None, :], far_scores, MASKED)
    page_max = jnp.max(far_scores, axis=3)
    far_weights = jnp.exp(far_scores - page_max[:, :, :, None])
    page_sum = jnp.sum(far_weights, axis=3)
    page_out = jnp.einsum(
        "phqk,pkhd->phqd",
        far_weights.astype(jnp.bfloat16),
        value_cache.reshape(page_count, page_len, head_count, HD),
        preferred_element_type=jnp.float32,
    )
    member_mask = owner_mask.T[:, :, None, None]
    dest_max = jnp.max(jnp.where(member_mask, page_max[None], MASKED), axis=1)
    factor = jnp.where(
        member_mask, jnp.exp(jnp.minimum(page_max[None] - dest_max[:, None], 0.0)), 0.0
    )
    dest_sum = jnp.einsum("rphq,phq->rhq", factor, page_sum, precision=HIGHEST)
    dest_out = jnp.einsum("rphq,phqd->rhqd", factor, page_out, precision=HIGHEST)
    got_out, got_max, got_sum = (
        lax.all_to_all(
            dest_out.astype(jnp.bfloat16), "seq", split_axis=0, concat_axis=0, tiled=True
        ).astype(dest_out.dtype),
        lax.all_to_all(
            dest_max.astype(jnp.bfloat16), "seq", split_axis=0, concat_axis=0, tiled=True
        ).astype(dest_max.dtype),
        lax.all_to_all(
            dest_sum.astype(jnp.bfloat16), "seq", split_axis=0, concat_axis=0, tiled=True
        ).astype(dest_sum.dtype),
    )
    own_queries = queries.reshape(draft_len, head_count, HD)
    near_scores = (
        jnp.einsum(
            "qhd,khd->hqk",
            own_queries,
            draft_keys.reshape(draft_len, head_count, HD),
            preferred_element_type=jnp.float32,
        )
        * scaling
    )
    near_scores = jnp.where((tree_mask[0] > 0)[None], near_scores, MASKED)
    near_max = jnp.max(near_scores, axis=2)
    near_weights = jnp.exp(near_scores - near_max[:, :, None])
    near_sum = jnp.sum(near_weights, axis=2)
    near_out = jnp.einsum(
        "hqk,khd->hqd",
        near_weights.astype(jnp.bfloat16),
        draft_values.reshape(draft_len, head_count, HD),
        preferred_element_type=jnp.float32,
    )
    row_max = jnp.maximum(near_max, jnp.max(got_max, axis=0))
    near_scale = jnp.exp(near_max - row_max)
    far_scale = jnp.exp(got_max - row_max[None])
    total_sum = near_sum * near_scale + jnp.sum(got_sum * far_scale, axis=0)
    summed = near_out * near_scale[:, :, None] + jnp.sum(got_out * far_scale[:, :, :, None], axis=0)
    attended = (
        (summed / total_sum[:, :, None])
        .transpose(1, 0, 2)
        .reshape(draft_len, head_width)
        .astype(jnp.bfloat16)
    )
    log_sum_exp = (row_max + jnp.log(total_sum)).T
    partial_proj = jnp.dot(attended, out_proj, preferred_element_type=jnp.float32)
    projected = lax.psum(partial_proj.astype(jnp.bfloat16), "tensor").astype(jnp.float32)
    mixed = hidden_in.astype(jnp.float32) + projected
    normed = (
        mixed * lax.rsqrt(jnp.mean(mixed * mixed, axis=1, keepdims=True) + 1e-06) * norm_gain
    ).astype(jnp.bfloat16)
    pick_count = expert_ids.shape[1]
    local_experts = gate_proj.shape[0]
    group_count = EXPERTS // local_experts
    slots_total = EXPERTS * CAP
    flat_ids = expert_ids.reshape(-1)
    hits = (flat_ids[:, None] == jnp.arange(EXPERTS, dtype=jnp.int32)[None, :]).astype(jnp.int32)
    rank = jnp.sum((jnp.cumsum(hits, axis=0) - hits) * hits, axis=1)
    slot_of = (flat_ids * CAP + rank).reshape(draft_len, pick_count)
    slot_ids = jnp.arange(slots_total, dtype=jnp.int32)
    dispatch_map = jnp.any(slot_ids[:, None, None] == slot_of[None], axis=2).astype(jnp.bfloat16)
    send_rows = (
        jnp.dot(dispatch_map, normed, preferred_element_type=jnp.float32)
        .astype(jnp.bfloat16)
        .reshape(group_count, local_experts, CAP, normed.shape[1])
    )
    combine = jnp.sum(
        jnp.where(slot_of[:, :, None] == slot_ids[None, None, :], route_weight[:, :, None], 0.0),
        axis=1,
    )
    column_width = mixed.shape[1] // lax.axis_size("tensor")
    column_start = lax.axis_index("tensor") * column_width
    result = expert_block(
        lax.all_to_all(send_rows, "seq", split_axis=0, concat_axis=0, tiled=True),
        gate_proj,
        up_proj,
        down_proj,
    )
    back_rows = lax.all_to_all(result, "seq", split_axis=0, concat_axis=0, tiled=True)
    flat_rows = back_rows.reshape(slots_total, back_rows.shape[3])
    combine_high = combine.astype(jnp.bfloat16)
    combine_low = (combine - combine_high.astype(jnp.float32)).astype(jnp.bfloat16)
    weighted = jnp.dot(combine_high, flat_rows, preferred_element_type=jnp.float32) + jnp.dot(
        combine_low, flat_rows, preferred_element_type=jnp.float32
    )
    moe_part = lax.psum_scatter(
        weighted.astype(jnp.bfloat16), "tensor", scatter_dimension=1, tiled=True
    ).astype(jnp.float32)
    mixed_out = (lax.dynamic_slice_in_dim(mixed, column_start, column_width, 1) + moe_part).astype(
        jnp.bfloat16
    )
    accept_count = every_accept.shape[1]
    page_accept = jnp.einsum(
        "pr,rac->pac", owner_weight, every_accept, preferred_element_type=jnp.float32
    ).astype(jnp.bfloat16)
    offset = position - page_length[:, None]
    placement = offset[:, :, None] == jnp.arange(accept_count, dtype=jnp.int32)[None, None, :]
    written = jnp.einsum(
        "pia,pac->pic",
        placement.astype(jnp.bfloat16),
        page_accept,
        preferred_element_type=jnp.float32,
    ).astype(jnp.bfloat16)
    touched = jnp.any(placement, axis=2)[:, :, None]
    key_cache_out = jnp.where(touched, written[:, :, :head_width], key_cache)
    value_cache_out = jnp.where(touched, written[:, :, head_width:], value_cache)
    return (mixed_out, log_sum_exp, key_cache_out, value_cache_out)


def solution(mesh):
    return jax.shard_map(
        on_device,
        mesh=mesh,
        in_specs=(
            P("seq", "tensor"),
            P("seq", "tensor"),
            P("seq", "tensor"),
            P("seq", None, "tensor"),
            P("seq", None, "tensor"),
            P("seq"),
            P("seq"),
            P(),
            P("seq", None, None),
            P("seq", None),
            P("seq", None),
            P("tensor", None),
            P(),
            P("seq", None, "tensor"),
            P("seq", None, "tensor"),
            P("seq", "tensor", None),
            P("seq", None),
            P("seq", None),
        ),
        out_specs=(
            P("seq", "tensor"),
            P("seq", "tensor"),
            P("seq", None, "tensor"),
            P("seq", None, "tensor"),
        ),
        check_vma=False,
    )
```

profile of v0, /device:TPU:0, one launch (start us, length us, event | category | flops | bytes accessed | tf_op | source)
XLA Modules:
  0.0 393.0 jit_solution(8291172530403849364)
XLA Ops:
  7.2 0.8 broadcast_multiply_fusion
  8.0 0.7 iota_compare_fusion.7
  8.6 0.8 select_reduce_fusion.2
  9.4 33.2 %all-gather = bf16[512,512]{1,0:T(8,128)(2,1)S(1)} all-gather(bf16[64,512]{1,0:T(8,128)(2,1)} %param.18), channel_id=2, replica_groups=mesh['seq'=8,'tensor'=4] {'seq'}, dimensions={0}, use_global_device_ids=true | all-gather | bytes 589824 | tf_op jit(solution)/shard_map/all_gather | solution.py:51
  42.6 1.2 convolution_convert_fusion.3
  43.8 1.3 reshape.247
  45.1 0.1 fusion.90
  45.1 4.0 %fusion.103 = (f32[12,4,64]{2,1,0:T(4,128)S(1)}, f32[12,4,64,128]{3,2,1,0:T(8,128)}) fusion(bf16[12,64,4,128]{3,2,0,1:T(4,128)(2,1)} %reshape.247, pred[12,128]{1,0:T(8,128)(4,1)S(1)} %fusion.90, bf16[12,128,512]{2,1,0:T(8,128)(2,1)} %param.21), kind=kOutput, calls=%fused_computation.125 | convolution fusion | flops 101839872 | bytes 3945984 | tf_op jit(solution)/shard_map/pqhd,pkhd->phqk/dot_general | solution.py:65
  49.1 0.1 copy.165
  49.2 2.3 fusion.22
  51.6 0.1 copy.197
  51.7 0.3 select_reduce_fusion.1
  52.0 0.7 multiply_reduce_fusion
  52.7 0.1 copy.206
  52.8 0.7 reshape.251
  53.5 5.7 %all-to-all-start.2 = ((bf16[8,2,128]{2,1,0:T(2,128)(2,1)}), bf16[8,2,128]{2,1,0:T(2,128)(2,1)S(1)}, u32[]{:S(2)}, u32[]{:S(2)}) async-start(bf16[8,2,128]{2,1,0:T(2,128)(2,1)} %reshape.251), calls=%async_computation.2 | async-start | bytes 8192 | tf_op jit(solution)/shard_map/all_to_all | solution.py:97
  59.2 0.1 copy.172
  59.3 0.1 eq.98
  59.3 0.1 eq.94
  59.5 2.5 fusion.14
  62.0 3.2 fusion.47
  65.2 1.2 reduce-window.6
  66.4 0.2 slice_reduce_fusion
  66.7 0.1 fusion.69
  66.8 0.1 copy.166
  66.9 0.7 reshape.249
  67.6 0.1 reduce_sum.89
  67.8 6.0 %all-to-all-start = ((bf16[8,2,128]{2,1,0:T(2,128)(2,1)}), bf16[8,2,128]{2,1,0:T(2,128)(2,1)S(1)}, u32[]{:S(2)}, u32[]{:S(2)}) async-start(bf16[8,2,128]{2,1,0:T(2,128)(2,1)} %reshape.249), calls=%async_computation | async-start | bytes 8192 | tf_op jit(solution)/shard_map/all_to_all | solution.py:94
  73.8 0.1 copy.156
  73.9 0.9 copy.170
  74.8 0.1 copy.176
  74.9 5.4 %all-to-all-done = bf16[8,2,128]{2,1,0:T(2,128)(2,1)S(1)} async-done(((bf16[8,2,128]{2,1,0:T(2,128)(2,1)}), bf16[8,2,128]{2,1,0:T(2,128)(2,1)S(1)}, u32[]{:S(2)}, u32[]{:S(2)}) %all-to-all-start) | async-done | bytes 4128 | tf_op jit(solution)/shard_map/all_to_all | solution.py:94
  80.3 3.5 all-to-all-start.1
  83.8 0.2 fusion.104
  84.1 0.1 reshape.250
  84.2 0.1 reshape.252
  84.3 0.6 fusion.95
  84.9 9.1 %all-to-all-done.1 = bf16[8,4,64,128]{3,2,1,0:T(8,128)(2,1)S(1)} async-done(((bf16[8,4,64,128]{3,2,1,0:T(8,128)(2,1)}), bf16[8,4,64,128]{3,2,1,0:T(8,128)(2,1)S(1)}, u32[]{:S(2)}, u32[]{:S(2)}) %all-to-all-start.1) | async-done | bytes 524320 | tf_op jit(solution)/shard_map/all_to_all | solution.py:91
  94.0 0.3 multiply_reduce_fusion.1
  94.3 0.2 fusion.55
  94.6 1.2 convolution_convert_fusion.1
  95.8 0.7 fusion.13
  96.5 30.5 %all-reduce.2.cloned.1.call-done = bf16[64,2048]{1,0:T(8,128)(2,1)} async-done(((bf16[64,2048]{1,0:T(8,128)(2,1)}), bf16[64,2048]{1,0:T(8,128)(2,1)}) %all-reduce.2.cloned.1.call-update) | async-done | bytes 262160 | tf_op jit(solution)/shard_map/psum | solution.py:134
  127.0 1.1 convert_add_fusion
  128.2 2.4 convolution_convert_fusion
  130.6 97.6 %all_to_all.25 = bf16[8,8,16,2048]{3,2,1,0:T(8,128)(2,1)S(1)} all-to-all(bf16[8,8,16,2048]{3,2,1,0:T(8,128)(2,1)S(1)} %bitcast.166), channel_id=1, replica_groups=mesh['seq'=8,'tensor'=4] {'seq'}, dimensions={0} | all-to-all | bytes 8388608 | tf_op jit(solution)/shard_map/all_to_all | solution.py:161
  228.3 1.3 fusion.24
  229.5 5.0 %fusion.39 = bf16[8,8,16,256]{3,2,0,1:T(8,128)(2,1)S(1)} fusion(bf16[8,2048,256]{2,1,0:T(8,128)(2,1)} %param.32, bf16[8,8,16,2048]{3,2,1,0:T(8,128)(2,1)S(1)} %all_to_all.25, f32[8,8,16,256]{3,2,0,1:T(8,128)S(1)} %fusion.24), kind=kOutput, calls=%fused_computation.38 | convolution fusion | flops 1075314688 | bytes 14155776 | tf_op jit(solution)/shard_map/gecd,edf->gecf/dot_general | solution.py:18
  234.6 1.3 convert_bitcast_fusion
  235.8 2.5 copy.181
  238.3 4.7 %all-to-all-start.4 = ((bf16[8,8,16,2048]{3,2,1,0:T(8,128)(2,1)}), bf16[8,8,16,2048]{3,2,1,0:T(8,128)(2,1)}, u32[]{:S(2)}, u32[]{:S(2)}) async-start(bf16[8,8,16,2048]{3,2,1,0:T(8,128)(2,1)} %copy.181), calls=%async_computation.4 | async-start | bytes 8388608 | tf_op jit(solution)/shard_map/all_to_all | solution.py:166
  243.1 0.6 gather_fusion
  243.7 0.6 gather_fusion.1
  244.3 0.1 copy.177
  244.3 110.9 %all-gather.1 = bf16[64,1024]{1,0:T(8,128)(2,1)S(1)} all-gather(bf16[8,1024]{1,0:T(8,128)(2,1)S(1)} %pad_maximum_fusion), channel_id=3, replica_groups=mesh['seq'=8,'tensor'=4] {'seq'}, dimensions={0}, use_global_device_ids=true | all-gather | bytes 147456 | tf_op jit(solution)/shard_map/all_gather | solution.py:52
  355.2 0.7 select_reduce_fusion
  355.9 0.1 fusion.89
  356.0 0.3 convolution_convert_fusion.4
  356.3 2.8 convolution_convert_fusion.2
  359.1 3.0 fusion.84
  362.1 3.7 fusion.10
  365.9 4.3 %slice_select_fusion = (bf16[12,128,512]{2,1,0:T(8,128)(2,1)}, bf16[12,128,512]{2,1,0:T(8,128)(2,1)}) fusion(bf16[12,128,512]{2,1,0:T(8,128)(2,1)} %param.22, bf16[12,128,1024]{2,1,0:T(8,128)(2,1)} %convolution_convert_fusion.2, pred[12,128]{1,0:T(8,128)(4,1)S(1)} %fusion.87, bf16[12,128,512]{2,1,0:T(8,128)(2,1)} %param.21), kind=kLoop, calls=%fused_computation.28 | loop fusion | flops 1572864 | bytes 9438720 | tf_op jit(solution)/shard_map/jit(_where)/select_n | solution.py:193
  370.2 14.5 %reduce-scatter.2.cloned.1.call-done = bf16[64,512]{1,0:T(8,128)(2,1)} async-done(((bf16[64,2048]{1,0:T(8,128)(2,1)}), bf16[64,512]{1,0:T(8,128)(2,1)}) %reduce-scatter.2.cloned.1.call-update) | async-done | bytes 65552 | tf_op jit(solution)/shard_map/reduce_scatter | solution.py:173
  384.7 1.5 add_convert_fusion
  (56 shorter events, 0.5 us)
Async XLA Ops:
  7.2 87.4 %copy-start = (bf16[512,2048]{1,0:T(8,128)(2,1)S(1)}, bf16[512,2048]{1,0:T(8,128)(2,1)}, u32[]{:S(2)}) copy-start(bf16[512,2048]{1,0:T(8,128)(2,1)} %param.29) | copy-start | bytes 6291460
  49.1 10.0 %copy-start.7 = (s32[64,8]{0,1:T(8,128)S(1)}, s32[64,8]{0,1:T(8,128)}, u32[]{:S(2)}) copy-start(s32[64,8]{0,1:T(8,128)} %param.34) | copy-start | bytes 6148
  49.1 10.3 %copy-start.6 = (s32[1,64,64]{2,1,0:T(8,128)S(1)}, s32[1,64,64]{2,1,0:T(8,128)}, u32[]{:S(2)}) copy-start(s32[1,64,64]{2,1,0:T(8,128)} %param.26) | copy-start | bytes 49156
  53.5 14.3 %all-to-all-start.2 = ((bf16[8,2,128]{2,1,0:T(2,128)(2,1)}), bf16[8,2,128]{2,1,0:T(2,128)(2,1)S(1)}, u32[]{:S(2)}, u32[]{:S(2)}) async-start(bf16[8,2,128]{2,1,0:T(2,128)(2,1)} %reshape.251), calls=%async_computation.2 | async-start | bytes 8192 | tf_op jit(solution)/shard_map/all_to_all | solution.py:97
  65.2 18.6 %copy-start.3 = (bf16[64,512]{1,0:T(8,128)(2,1)S(1)}, bf16[64,512]{1,0:T(8,128)(2,1)}, u32[]{:S(2)}) copy-start(bf16[64,512]{1,0:T(8,128)(2,1)} %param.18) | copy-start | bytes 196612
  65.2 18.6 %copy-start.4 = (bf16[64,512]{1,0:T(8,128)(2,1)S(1)}, bf16[64,512]{1,0:T(8,128)(2,1)}, u32[]{:S(2)}) copy-start(bf16[64,512]{1,0:T(8,128)(2,1)} %param.19) | copy-start | bytes 196612
  65.2 29.1 %copy-start.5 = (bf16[64,512]{1,0:T(8,128)(2,1)S(1)}, bf16[64,512]{1,0:T(8,128)(2,1)}, u32[]{:S(2)}) copy-start(bf16[64,512]{1,0:T(8,128)(2,1)} %param.20) | copy-start | bytes 196612
  67.8 12.5 %all-to-all-start = ((bf16[8,2,128]{2,1,0:T(2,128)(2,1)}), bf16[8,2,128]{2,1,0:T(2,128)(2,1)S(1)}, u32[]{:S(2)}, u32[]{:S(2)}) async-start(bf16[8,2,128]{2,1,0:T(2,128)(2,1)} %reshape.249), calls=%async_computation | async-start | bytes 8192 | tf_op jit(solution)/shard_map/all_to_all | solution.py:94
  80.3 13.7 %all-to-all-start.1 = ((bf16[8,4,64,128]{3,2,1,0:T(8,128)(2,1)}), bf16[8,4,64,128]{3,2,1,0:T(8,128)(2,1)S(1)}, u32[]{:S(2)}, u32[]{:S(2)}) async-start(bf16[8,4,64,128]{3,2,1,0:T(8,128)(2,1)} %copy.170), calls=%async_computation.1 | async-start | bytes 1048576 | tf_op jit(solution)/shard_map/all_to_all | solution.py:91
  83.8 43.3 %all-reduce.2.cloned.1.call-start = ((), (), s32[]{:S(2)}) async-start(), calls=%async_computation.6 | async-start | bytes 524288 | tf_op jit(solution)/shard_map/psum | solution.py:134
  84.3 42.8 %copy-start.2 = (bf16[64,2048]{1,0:T(8,128)(2,1)S(1)}, bf16[64,2048]{1,0:T(8,128)(2,1)}, u32[]{:S(2)}) copy-start(bf16[64,2048]{1,0:T(8,128)(2,1)} %param.28) | copy-start | bytes 786436
  94.3 33.9 %copy-start.8 = (f32[2048]{0:T(1024)S(1)}, f32[2048]{0:T(1024)}, u32[]{:S(2)}) copy-start(f32[2048]{0:T(1024)} %param.30) | copy-start | bytes 24580
  128.2 100.1 %slice-start.2 = ((s8[8388608]{0:T(1024)(128)(4,1)}), s8[4194304]{0:T(1024)(128)(4,1)S(1)}, s32[]{:S(2)}) async-start(s8[8388608]{0:T(1024)(128)(4,1)} %bitcast.173), calls=%async_computation.10 | async-start | bytes 8388608
  130.6 97.6 %slice-start.3 = ((s8[8388608]{0:T(1024)(128)(4,1)}), s8[4194304]{0:T(1024)(128)(4,1)S(1)}, s32[]{:S(2)}) async-start(s8[8388608]{0:T(1024)(128)(4,1)} %bitcast.173), calls=%async_computation.11 | async-start | bytes 8388608
  228.3 6.3 %slice-start = ((s8[8388608]{0:T(1024)(128)(4,1)}), s8[4194304]{0:T(1024)(128)(4,1)S(1)}, s32[]{:S(2)}) async-start(s8[8388608]{0:T(1024)(128)(4,1)} %bitcast.167), calls=%async_computation.8 | async-start | bytes 8388608
  229.5 5.0 %slice-start.1 = ((s8[8388608]{0:T(1024)(128)(4,1)}), s8[4194304]{0:T(1024)(128)(4,1)S(1)}, s32[]{:S(2)}) async-start(s8[8388608]{0:T(1024)(128)(4,1)} %bitcast.167), calls=%async_computation.9 | async-start | bytes 8388608
  238.3 4.7 %copy-start.11 = (s32[1,8]{1,0:T(1,128)S(1)}, s32[1,8]{1,0:T(1,128)}, u32[]{:S(2)}) copy-start(s32[1,8]{1,0:T(1,128)} %param.27) | copy-start | bytes 100
  238.3 5.9 %copy-start.9 = (f32[64,8]{0,1:T(8,128)S(1)}, f32[64,8]{0,1:T(8,128)}, u32[]{:S(2)}) copy-start(f32[64,8]{0,1:T(8,128)} %param.35) | copy-start | bytes 6148
  238.3 117.7 %copy-start.10 = (s32[12]{0:T(128)S(1)}, s32[12]{0:T(128)}, u32[]{:S(2)}) copy-start(s32[12]{0:T(128)} %param.23) | copy-start | bytes 148
  238.3 120.8 %all-to-all-start.4 = ((bf16[8,8,16,2048]{3,2,1,0:T(8,128)(2,1)}), bf16[8,8,16,2048]{3,2,1,0:T(8,128)(2,1)}, u32[]{:S(2)}, u32[]{:S(2)}) async-start(bf16[8,8,16,2048]{3,2,1,0:T(8,128)(2,1)} %copy.181), calls=%async_computation.4 | async-start | bytes 8388608 | tf_op jit(solution)/shard_map/all_to_all | solution.py:166
  243.0 141.7 %reduce-scatter.2.cloned.1.call-start = ((), (), s32[]{:S(2)}) async-start(), calls=%async_computation.7 | async-start | bytes 327680 | tf_op jit(solution)/shard_map/reduce_scatter | solution.py:173
  365.9 20.3 %copy-start.1 = (bf16[512,2048]{1,0:T(8,128)(2,1)S(1)}, bf16[512,2048]{1,0:T(8,128)(2,1)}, u32[]{:S(2)}) copy-start(bf16[512,2048]{1,0:T(8,128)(2,1)} %param.29) | copy-start | bytes 6291460
Sparse Core Ops, SparseCore 0:
  95.9 31.0 all-reduce.1
  366.0 18.6 reduce-scatter.1
where the time goes:
time: 394 us; the launch traced here: 393 us
  blocking collectives  242 us (61%)
  waiting for transfers between devices  59.5 us (15%)
  matrix products  32.2 us (8%)
  starting transfers between devices  19.9 us (5%)
  other arithmetic  16.5 us (4%)
  between operations  14.4 us (4%)
  local copies, waits for them, and re-layouts  8.74 us (2%)
    all_gather x1, blocking collectives, on_device(): lax.all_gather(accept_rows[None], 'seq', axis=0, tiled=True)  111 us
    all_to_all x1, blocking collectives, on_device(): lax.all_to_all(send_rows, 'seq', split_axis=0, concat_axis=0, tiled=True)  97.6 us
    all_gather x1, blocking collectives, on_device(): lax.all_gather(queries[None], 'seq', axis=0, tiled=True)  33.2 us
    psum x1, waiting for transfers between devices, on_device(): lax.psum(partial_proj.astype(jnp.bfloat16), 'tensor').astype(jnp.float32)  30.5 us
    reduce_scatter x1, waiting for transfers between devices, on_device(): lax.psum_scatter(weighted.astype(jnp.bfloat16), 'tensor', scatter_dimensi...  14.5 us
    all_to_all x1, waiting for transfers between devices, on_device(): lax.all_to_all(dest_out.astype(jnp.bfloat16), 'seq', split_axis=0, concat...  9.08 us
  transfers between devices with their start and end apart: 6, of which 4 were waited for; matrix products, arithmetic and copies ran while one was open for 5% of the time, Pallas kernels for 0%

commit v1 on v0

--- a/solution.py
+++ b/solution.py
@@ -131,7 +131,9 @@
     )
     log_sum_exp = (row_max + jnp.log(total_sum)).T
     partial_proj = jnp.dot(attended, out_proj, preferred_element_type=jnp.float32)
-    projected = lax.psum(partial_proj.astype(jnp.bfloat16), "tensor").astype(jnp.float32)
+    projected = jnp.sum(lax.all_gather(partial_proj.astype(jnp.bfloat16), "tensor"), axis=0).astype(
+        jnp.float32
+    )
     mixed = hidden_in.astype(jnp.float32) + projected
     normed = (
         mixed * lax.rsqrt(jnp.mean(mixed * mixed, axis=1, keepdims=True) + 1e-06) * norm_gain

time: 394 us -> 377 us (0.957)
  waiting for transfers between devices: 59.5 us -> 41.6 us
    psum x1 -> x0, waiting for transfers between devices: 30.5 us -> none  [on_device(): lax.psum(partial_proj.astype(jnp.bfloat16), 'tensor').astype(jnp.float32)]
    all_gather x0 -> x1, waiting for transfers between devices: none -> 13.1 us  [on_device(): lax.all_gather(partial_proj.astype(jnp.bfloat16), 'tensor')]
  transfers between devices with their start and end apart: 6 -> 6, of which waited for: 4 -> 4; matrix products, arithmetic and copies ran while one was open for 5% -> 6% of each run, Pallas kernels for 0% -> 0%
where the time goes in v1:
time: 377 us; the launch traced here: 376 us
  blocking collectives  244 us (65%)
  waiting for transfers between devices  41.6 us (11%)
  matrix products  31.1 us (8%)
  starting transfers between devices  19.9 us (5%)
  other arithmetic  17 us (5%)
  between operations  14.4 us (4%)
  local copies, waits for them, and re-layouts  8.76 us (2%)
    all_gather x1, blocking collectives, on_device(): lax.all_gather(accept_rows[None], 'seq', axis=0, tiled=True)  111 us
    all_to_all x1, blocking collectives, on_device(): lax.all_to_all(send_rows, 'seq', split_axis=0, concat_axis=0, tiled=True)  99.1 us
    all_gather x1, blocking collectives, on_device(): lax.all_gather(queries[None], 'seq', axis=0, tiled=True)  33.2 us
    reduce_scatter x1, waiting for transfers between devices, on_device(): lax.psum_scatter(weighted.astype(jnp.bfloat16), 'tensor', scatter_dimensi...  13.9 us
    all_gather x1, waiting for transfers between devices, on_device(): lax.all_gather(partial_proj.astype(jnp.bfloat16), 'tensor')  13.1 us
    all_to_all x1, waiting for transfers between devices, on_device(): lax.all_to_all(dest_out.astype(jnp.bfloat16), 'seq', split_axis=0, concat...  9.07 us
  transfers between devices with their start and end apart: 6, of which 4 were waited for; matrix products, arithmetic and copies ran while one was open for 6% of the time, Pallas kernels for 0%

profile of v1, /device:TPU:0, one launch (start us, length us, event | category | flops | bytes accessed | tf_op | source)
XLA Modules:
  0.0 376.3 jit_solution(9274206276186860830)
XLA Ops:
  7.2 0.8 broadcast_multiply_fusion
  8.0 0.7 iota_compare_fusion.7
  8.6 0.8 select_reduce_fusion.2
  9.4 33.2 %all-gather = bf16[512,512]{1,0:T(8,128)(2,1)S(1)} all-gather(bf16[64,512]{1,0:T(8,128)(2,1)} %param.18), channel_id=2, replica_groups=mesh['seq'=8,'tensor'=4] {'seq'}, dimensions={0}, use_global_device_ids=true | all-gather | bytes 589824 | tf_op jit(solution)/shard_map/all_gather | solution.py:51
  42.6 1.2 convolution_convert_fusion.3
  43.8 1.3 reshape.248
  45.1 0.1 fusion.90
  45.1 4.0 %fusion.103 = (f32[12,4,64]{2,1,0:T(4,128)S(1)}, f32[12,4,64,128]{3,2,1,0:T(8,128)}) fusion(bf16[12,64,4,128]{3,2,0,1:T(4,128)(2,1)} %reshape.248, pred[12,128]{1,0:T(8,128)(4,1)S(1)} %fusion.90, bf16[12,128,512]{2,1,0:T(8,128)(2,1)} %param.21), kind=kOutput, calls=%fused_computation.125 | convolution fusion | flops 101839872 | bytes 3945984 | tf_op jit(solution)/shard_map/pqhd,pkhd->phqk/dot_general | solution.py:65
  49.1 0.1 copy.165
  49.2 2.3 fusion.22
  51.6 0.1 copy.197
  51.7 0.3 select_reduce_fusion.1
  52.0 0.7 multiply_reduce_fusion
  52.7 0.1 copy.206
  52.8 0.7 reshape.252
  53.5 5.7 %all-to-all-start.2 = ((bf16[8,2,128]{2,1,0:T(2,128)(2,1)}), bf16[8,2,128]{2,1,0:T(2,128)(2,1)S(1)}, u32[]{:S(2)}, u32[]{:S(2)}) async-start(bf16[8,2,128]{2,1,0:T(2,128)(2,1)} %reshape.252), calls=%async_computation.2 | async-start | bytes 8192 | tf_op jit(solution)/shard_map/all_to_all | solution.py:97
  59.2 2.5 fusion.14
  61.7 3.2 fusion.47
  64.9 0.1 copy.166
  65.0 0.7 reshape.250
  65.7 6.0 %all-to-all-start = ((bf16[8,2,128]{2,1,0:T(2,128)(2,1)}), bf16[8,2,128]{2,1,0:T(2,128)(2,1)S(1)}, u32[]{:S(2)}, u32[]{:S(2)}) async-start(bf16[8,2,128]{2,1,0:T(2,128)(2,1)} %reshape.250), calls=%async_computation | async-start | bytes 8192 | tf_op jit(solution)/shard_map/all_to_all | solution.py:94
  71.7 0.1 copy.156
  71.8 0.9 copy.170
  72.7 5.4 %all-to-all-done = bf16[8,2,128]{2,1,0:T(2,128)(2,1)S(1)} async-done(((bf16[8,2,128]{2,1,0:T(2,128)(2,1)}), bf16[8,2,128]{2,1,0:T(2,128)(2,1)S(1)}, u32[]{:S(2)}, u32[]{:S(2)}) %all-to-all-start) | async-done | bytes 4128 | tf_op jit(solution)/shard_map/all_to_all | solution.py:94
  78.2 3.5 all-to-all-start.1
  81.7 0.2 fusion.104
  82.0 0.1 reshape.251
  82.1 0.1 reshape.253
  82.2 0.6 fusion.95
  82.8 9.1 %all-to-all-done.1 = bf16[8,4,64,128]{3,2,1,0:T(8,128)(2,1)S(1)} async-done(((bf16[8,4,64,128]{3,2,1,0:T(8,128)(2,1)}), bf16[8,4,64,128]{3,2,1,0:T(8,128)(2,1)S(1)}, u32[]{:S(2)}, u32[]{:S(2)}) %all-to-all-start.1) | async-done | bytes 524320 | tf_op jit(solution)/shard_map/all_to_all | solution.py:91
  91.9 0.3 multiply_reduce_fusion.1
  92.2 0.2 fusion.55
  92.5 1.2 convolution_convert_fusion.1
  93.7 0.1 copy.172
  93.8 0.1 eq.98
  93.9 0.1 eq.94
  94.0 1.2 reduce-window.6
  95.2 0.2 slice_reduce_fusion
  95.5 0.1 fusion.69
  95.6 0.1 reduce_sum.102
  95.8 0.1 copy.176
  95.9 0.7 fusion.13
  96.6 13.1 %all-gather.5.cloned.1.call-done = bf16[256,2048]{1,0:T(8,128)(2,1)} async-done(((bf16[64,2048]{1,0:T(8,128)(2,1)}), bf16[256,2048]{1,0:T(8,128)(2,1)}) %all-gather.5.cloned.1.call-update) | async-done | bytes 1048592 | tf_op jit(solution)/shard_map/all_gather | solution.py:134
  109.7 1.4 reduce_sum.100
  111.1 0.2 convert_add_fusion
  111.3 1.3 convolution_convert_fusion
  112.6 99.1 %all_to_all.25 = bf16[8,8,16,2048]{3,2,1,0:T(8,128)(2,1)S(1)} all-to-all(bf16[8,8,16,2048]{3,2,1,0:T(8,128)(2,1)S(1)} %bitcast.167), channel_id=1, replica_groups=mesh['seq'=8,'tensor'=4] {'seq'}, dimensions={0} | all-to-all | bytes 8388608 | tf_op jit(solution)/shard_map/all_to_all | solution.py:163
  211.8 1.3 fusion.24
  213.0 5.0 %fusion.39 = bf16[8,8,16,256]{3,2,0,1:T(8,128)(2,1)S(1)} fusion(bf16[8,2048,256]{2,1,0:T(8,128)(2,1)} %param.32, bf16[8,8,16,2048]{3,2,1,0:T(8,128)(2,1)S(1)} %all_to_all.25, f32[8,8,16,256]{3,2,0,1:T(8,128)S(1)} %fusion.24), kind=kOutput, calls=%fused_computation.38 | convolution fusion | flops 1075314688 | bytes 14155776 | tf_op jit(solution)/shard_map/gecd,edf->gecf/dot_general | solution.py:18
  218.1 1.3 convert_bitcast_fusion
  219.3 2.5 copy.181
  221.8 4.7 %all-to-all-start.4 = ((bf16[8,8,16,2048]{3,2,1,0:T(8,128)(2,1)}), bf16[8,8,16,2048]{3,2,1,0:T(8,128)(2,1)}, u32[]{:S(2)}, u32[]{:S(2)}) async-start(bf16[8,8,16,2048]{3,2,1,0:T(8,128)(2,1)} %copy.181), calls=%async_computation.4 | async-start | bytes 8388608 | tf_op jit(solution)/shard_map/all_to_all | solution.py:168
  226.6 0.6 gather_fusion
  227.2 0.6 gather_fusion.1
  227.8 0.1 copy.177
  227.8 111.2 %all-gather.2 = bf16[64,1024]{1,0:T(8,128)(2,1)S(1)} all-gather(bf16[8,1024]{1,0:T(8,128)(2,1)S(1)} %pad_maximum_fusion), channel_id=4, replica_groups=mesh['seq'=8,'tensor'=4] {'seq'}, dimensions={0}, use_global_device_ids=true | all-gather | bytes 147456 | tf_op jit(solution)/shard_map/all_gather | solution.py:52
  339.0 0.7 select_reduce_fusion
  339.8 0.3 convolution_convert_fusion.4
  340.1 2.8 convolution_convert_fusion.2
  342.9 3.0 fusion.84
  345.9 3.7 fusion.10
  349.7 4.3 %slice_select_fusion = (bf16[12,128,512]{2,1,0:T(8,128)(2,1)}, bf16[12,128,512]{2,1,0:T(8,128)(2,1)}) fusion(bf16[12,128,512]{2,1,0:T(8,128)(2,1)} %param.22, bf16[12,128,1024]{2,1,0:T(8,128)(2,1)} %convolution_convert_fusion.2, pred[12,128]{1,0:T(8,128)(4,1)S(1)} %fusion.87, bf16[12,128,512]{2,1,0:T(8,128)(2,1)} %param.21), kind=kLoop, calls=%fused_computation.28 | loop fusion | flops 1572864 | bytes 9438720 | tf_op jit(solution)/shard_map/jit(_where)/select_n | solution.py:195
  354.0 13.9 %reduce-scatter.2.cloned.1.call-done = bf16[64,512]{1,0:T(8,128)(2,1)} async-done(((bf16[64,2048]{1,0:T(8,128)(2,1)}), bf16[64,512]{1,0:T(8,128)(2,1)}) %reduce-scatter.2.cloned.1.call-update) | async-done | bytes 65552 | tf_op jit(solution)/shard_map/reduce_scatter | solution.py:175
  368.0 1.5 add_convert_fusion
  (57 shorter events, 0.6 us)
Async XLA Ops:
  7.2 85.3 %copy-start = (bf16[512,2048]{1,0:T(8,128)(2,1)S(1)}, bf16[512,2048]{1,0:T(8,128)(2,1)}, u32[]{:S(2)}) copy-start(bf16[512,2048]{1,0:T(8,128)(2,1)} %param.29) | copy-start | bytes 6291460
  53.5 12.2 %all-to-all-start.2 = ((bf16[8,2,128]{2,1,0:T(2,128)(2,1)}), bf16[8,2,128]{2,1,0:T(2,128)(2,1)S(1)}, u32[]{:S(2)}, u32[]{:S(2)}) async-start(bf16[8,2,128]{2,1,0:T(2,128)(2,1)} %reshape.252), calls=%async_computation.2 | async-start | bytes 8192 | tf_op jit(solution)/shard_map/all_to_all | solution.py:97
  61.6 10.0 %copy-start.6 = (s32[1,64,64]{2,1,0:T(8,128)S(1)}, s32[1,64,64]{2,1,0:T(8,128)}, u32[]{:S(2)}) copy-start(s32[1,64,64]{2,1,0:T(8,128)} %param.26) | copy-start | bytes 49156
  61.7 20.1 %copy-start.3 = (bf16[64,512]{1,0:T(8,128)(2,1)S(1)}, bf16[64,512]{1,0:T(8,128)(2,1)}, u32[]{:S(2)}) copy-start(bf16[64,512]{1,0:T(8,128)(2,1)} %param.18) | copy-start | bytes 196612
  61.7 20.1 %copy-start.4 = (bf16[64,512]{1,0:T(8,128)(2,1)S(1)}, bf16[64,512]{1,0:T(8,128)(2,1)}, u32[]{:S(2)}) copy-start(bf16[64,512]{1,0:T(8,128)(2,1)} %param.19) | copy-start | bytes 196612
  64.9 27.3 %copy-start.5 = (bf16[64,512]{1,0:T(8,128)(2,1)S(1)}, bf16[64,512]{1,0:T(8,128)(2,1)}, u32[]{:S(2)}) copy-start(bf16[64,512]{1,0:T(8,128)(2,1)} %param.20) | copy-start | bytes 196612
  65.7 12.5 %all-to-all-start = ((bf16[8,2,128]{2,1,0:T(2,128)(2,1)}), bf16[8,2,128]{2,1,0:T(2,128)(2,1)S(1)}, u32[]{:S(2)}, u32[]{:S(2)}) async-start(bf16[8,2,128]{2,1,0:T(2,128)(2,1)} %reshape.250), calls=%async_computation | async-start | bytes 8192 | tf_op jit(solution)/shard_map/all_to_all | solution.py:94
  78.2 13.7 %all-to-all-start.1 = ((bf16[8,4,64,128]{3,2,1,0:T(8,128)(2,1)}), bf16[8,4,64,128]{3,2,1,0:T(8,128)(2,1)S(1)}, u32[]{:S(2)}, u32[]{:S(2)}) async-start(bf16[8,4,64,128]{3,2,1,0:T(8,128)(2,1)} %copy.170), calls=%async_computation.1 | async-start | bytes 1048576 | tf_op jit(solution)/shard_map/all_to_all | solution.py:91
  81.7 28.0 %all-gather.5.cloned.1.call-start = ((), (), s32[]{:S(2)}) async-start(), calls=%async_computation.7 | async-start | bytes 1310720 | tf_op jit(solution)/shard_map/all_gather | solution.py:134
  82.0 11.7 %copy-start.7 = (s32[64,8]{0,1:T(8,128)S(1)}, s32[64,8]{0,1:T(8,128)}, u32[]{:S(2)}) copy-start(s32[64,8]{0,1:T(8,128)} %param.34) | copy-start | bytes 6148
  92.5 18.6 %copy-start.2 = (bf16[64,2048]{1,0:T(8,128)(2,1)S(1)}, bf16[64,2048]{1,0:T(8,128)(2,1)}, u32[]{:S(2)}) copy-start(bf16[64,2048]{1,0:T(8,128)(2,1)} %param.28) | copy-start | bytes 786436
  93.7 17.6 %copy-start.8 = (f32[2048]{0:T(1024)S(1)}, f32[2048]{0:T(1024)}, u32[]{:S(2)}) copy-start(f32[2048]{0:T(1024)} %param.30) | copy-start | bytes 24580
  111.3 100.5 %slice-start.2 = ((s8[8388608]{0:T(1024)(128)(4,1)}), s8[4194304]{0:T(1024)(128)(4,1)S(1)}, s32[]{:S(2)}) async-start(s8[8388608]{0:T(1024)(128)(4,1)} %bitcast.175), calls=%async_computation.10 | async-start | bytes 8388608
  112.6 99.1 %slice-start.3 = ((s8[8388608]{0:T(1024)(128)(4,1)}), s8[4194304]{0:T(1024)(128)(4,1)S(1)}, s32[]{:S(2)}) async-start(s8[8388608]{0:T(1024)(128)(4,1)} %bitcast.175), calls=%async_computation.11 | async-start | bytes 8388608
  211.8 6.3 %slice-start = ((s8[8388608]{0:T(1024)(128)(4,1)}), s8[4194304]{0:T(1024)(128)(4,1)S(1)}, s32[]{:S(2)}) async-start(s8[8388608]{0:T(1024)(128)(4,1)} %bitcast.168), calls=%async_computation.8 | async-start | bytes 8388608
  213.0 5.0 %slice-start.1 = ((s8[8388608]{0:T(1024)(128)(4,1)}), s8[4194304]{0:T(1024)(128)(4,1)S(1)}, s32[]{:S(2)}) async-start(s8[8388608]{0:T(1024)(128)(4,1)} %bitcast.168), calls=%async_computation.9 | async-start | bytes 8388608
  221.8 4.7 %copy-start.11 = (s32[1,8]{1,0:T(1,128)S(1)}, s32[1,8]{1,0:T(1,128)}, u32[]{:S(2)}) copy-start(s32[1,8]{1,0:T(1,128)} %param.27) | copy-start | bytes 100
  221.8 5.9 %copy-start.9 = (f32[64,8]{0,1:T(8,128)S(1)}, f32[64,8]{0,1:T(8,128)}, u32[]{:S(2)}) copy-start(f32[64,8]{0,1:T(8,128)} %param.35) | copy-start | bytes 6148
  221.8 118.0 %copy-start.10 = (s32[12]{0:T(128)S(1)}, s32[12]{0:T(128)}, u32[]{:S(2)}) copy-start(s32[12]{0:T(128)} %param.23) | copy-start | bytes 148
  221.8 121.1 %all-to-all-start.4 = ((bf16[8,8,16,2048]{3,2,1,0:T(8,128)(2,1)}), bf16[8,8,16,2048]{3,2,1,0:T(8,128)(2,1)}, u32[]{:S(2)}, u32[]{:S(2)}) async-start(bf16[8,8,16,2048]{3,2,1,0:T(8,128)(2,1)} %copy.181), calls=%async_computation.4 | async-start | bytes 8388608 | tf_op jit(solution)/shard_map/all_to_all | solution.py:168
  226.5 141.5 %reduce-scatter.2.cloned.1.call-start = ((), (), s32[]{:S(2)}) async-start(), calls=%async_computation.6 | async-start | bytes 327680 | tf_op jit(solution)/shard_map/reduce_scatter | solution.py:175
  349.7 19.7 %copy-start.1 = (bf16[512,2048]{1,0:T(8,128)(2,1)S(1)}, bf16[512,2048]{1,0:T(8,128)(2,1)}, u32[]{:S(2)}) copy-start(bf16[512,2048]{1,0:T(8,128)(2,1)} %param.29) | copy-start | bytes 6291460
Sparse Core Ops, SparseCore 0:
  93.8 15.8 all-gather.4
  349.8 18.1 reduce-scatter.1
